TPU v7x, 32 devices: a whole 2x2x4 slice. The times are simulated.
32 devices in a mesh: groups: 2 (over y), builds: 16 (over z, x, core).
Axes of the slice: x: 2, y: 2, z: 4, core: 2. Of those that a mesh axis runs over, the one named last changes fastest.
Arguments:
- build_factors: bfloat16 [393216, 256], P('builds')
- nz_build: int32 [16384], P(('groups', 'builds')), parts along dimension 0, may hold values from 0 to 24575
- nz_test: int32 [16384, 1], P(('groups', 'builds')), parts along dimension 0, may hold values from 0 to 255; in each aligned block of 512 rows (0 to 511, 512 to 1023, ...) at most 4 rows name the same one
- nz_count: int32 [16384], P(('groups', 'builds')), parts along dimension 0, may hold values from 1 to 15
- start_factors: float32 [512, 256], P(('groups', 'builds')), parts along dimension 0, may hold values from -6 to 6
Outputs:
- test_factors: float32 [512, 256], P(('groups', 'builds')), parts along dimension 0
There are 2 independent parts, one for each index of `groups`. A program takes and returns all parts, laid end to end along the dimension named above; an argument that names none is the same for every part. Nothing has to cross between parts.
Inputs may be any that keep to these rules, and one draw needn't show every extreme that they name: `nz_test`: among the nonzeros of one device no test appears more than 4 times, and on every device some test appears exactly 4 times.
All inputs are finite; a program needn't handle non-finite values.
Results may differ from a plain program's by a relative error of at most 0.0003.
Values may be sent and summed in bfloat16 or wider, within the bound.
A program may use at most 64 MiB of HBM per device.

v0:
```python
import jax
import jax.numpy as jnp
from jax import lax
from jax.sharding import PartitionSpec as P

ITERS = 3


epsilon = 1e-06


def shards(build_factors, nz_build, nz_test, nz_count, start_factors):
    test_rows, rank_dim = start_factors.shape
    bld_rows = build_factors.shape[0]
    nz_rows = nz_build.shape[0]
    devices = lax.axis_size("builds")
    tests_all = test_rows * devices
    conf_scale = devices * bld_rows * test_rows / (8.0 * nz_rows)
    damping = 0.4 * conf_scale
    gram_local = lax.dot_general(
        build_factors, build_factors, (((0,), (0,)), ((), ())), preferred_element_type=jnp.float32
    )
    test_ids = nz_test[:, 0]
    weight = conf_scale * nz_count.astype(jnp.float32)
    picked_rows = build_factors[nz_build]

    def sparse_apply(factors, with_target):
        gathered = lax.all_gather(factors, "builds", axis=0, tiled=True)
        wide_rows = picked_rows.astype(jnp.float32)
        inner_vals = jnp.sum(wide_rows * gathered[test_ids], axis=1)
        coeffs = weight * (1.0 - inner_vals) if with_target else weight * inner_vals
        partial_value = jax.ops.segment_sum(
            coeffs[:, None] * wide_rows, test_ids, num_segments=tests_all
        )
        return lax.psum_scatter(partial_value, "builds", scatter_dimension=0, tiled=True)

    shared = lax.psum(gram_local, "builds")

    def dense_part(field):
        return jnp.dot(field, shared, precision=lax.Precision.HIGHEST) + damping * field

    factors = start_factors
    residual = sparse_apply(start_factors, True) - dense_part(start_factors)
    direction = residual
    norm_now = jnp.sum(residual * residual, axis=1)
    for sweep_idx in range(ITERS):
        image_vec = sparse_apply(direction, False) + dense_part(direction)
        step_size = norm_now / (jnp.sum(direction * image_vec, axis=1) + epsilon)
        factors = factors + step_size[:, None] * direction
        if sweep_idx + 1 < ITERS:
            residual = residual - step_size[:, None] * image_vec
            norm_next = jnp.sum(residual * residual, axis=1)
            direction = residual + (norm_next / (norm_now + epsilon))[:, None] * direction
            norm_now = norm_next
    return factors


def solution(mesh):
    return jax.shard_map(
        shards,
        mesh=mesh,
        in_specs=(
            P("builds", None),
            P(("groups", "builds")),
            P(("groups", "builds"), None),
            P(("groups", "builds")),
            P(("groups", "builds"), None),
        ),
        out_specs=P(("groups", "builds"), None),
        check_vma=False,
    )
```

profile of v0, /device:TPU:0, one launch (start us, length us, event | category | flops | bytes accessed | tf_op | source)
XLA Modules:
  0.0 418.8 jit_solution(1950160589801684431)
XLA Ops:
  6.5 0.0 copy-start.3
  6.5 0.0 copy-start.4
  6.5 0.0 copy-start.1
  6.5 0.0 copy-start.2
  6.5 0.0 all-reduce.2.cloned.1.call-start
  6.6 12.3 %fusion.26 = f32[256,256]{1,0:T(8,128)} fusion(bf16[24576,256]{1,0:T(8,128)(2,1)} %param.5), kind=kOutput, calls=%fused_computation.68 | convolution fusion | flops 3221225472 | bytes 12845056 | tf_op jit(solution)/shard_map/dot_general | solution.py:20
  18.9 0.0 all-reduce.2.cloned.1.call-update
  19.0 0.0 reduce-scatter.5.cloned.1.call-start
  19.0 0.0 copy-done.3
  19.0 0.0 copy-done.4
  19.1 7.8 %gather_fusion = bf16[512,256]{1,0:T(8,128)(2,1)S(1)} fusion(bf16[24576,256]{1,0:T(8,128)(2,1)} %param.5, s32[1024]{0:T(1024)S(1)} %pad_clamp_fusion.1), kind=kCustom, calls=%fused_computation | custom fusion | bytes 526336 | tf_op jit(solution)/shard_map/gather | solution.py:25
  26.8 0.0 copy-done.1
  26.8 23.9 %all_gather.12 = f32[256,256]{1,0:T(8,128)S(1)} all-gather(f32[16,256]{1,0:T(8,128)S(1)} %copy-done.1), channel_id=1, replica_groups=mesh['groups'=2,'builds'=16] {'builds'}, dimensions={0}, use_global_device_ids=true | all-gather | bytes 278528 | tf_op jit(solution)/shard_map/all_gather | solution.py:28
  50.8 1.6 gather_fusion.1
  52.4 0.2 fusion.7
  52.5 0.0 copy-done.2
  52.5 4.1 scatter_custom_fusion
  56.6 0.0 reduce-scatter.5.cloned.1.call-update
  56.7 0.0 reduce-scatter.7.cloned.1.call-start
  56.7 53.9 %all-reduce.2.cloned.1.call-done = f32[256,256]{1,0:T(8,128)} async-done(((f32[256,256]{1,0:T(8,128)}), f32[256,256]{1,0:T(8,128)}) %all-reduce.2.cloned.1.call-update) | async-done | bytes 262160 | tf_op jit(solution)/shard_map/psum | solution.py:37
  110.7 0.0 copy-start
  110.7 59.3 %reduce-scatter.5.cloned.1.call-done = f32[16,256]{1,0:T(8,128)} async-done(((f32[256,256]{1,0:T(8,128)}), f32[16,256]{1,0:T(8,128)}) %reduce-scatter.5.cloned.1.call-update) | async-done | bytes 16400 | tf_op jit(solution)/shard_map/reduce_scatter | solution.py:35
  170.0 1.2 fusion.5
  171.2 20.3 %all_gather.13 = f32[256,256]{1,0:T(8,128)S(1)} all-gather(f32[16,256]{1,0:T(8,128)S(1)} %fusion.5), channel_id=1, replica_groups=mesh['groups'=2,'builds'=16] {'builds'}, dimensions={0}, use_global_device_ids=true | all-gather | bytes 278528 | tf_op jit(solution)/shard_map/all_gather | solution.py:28
  191.5 1.6 gather_fusion.2
  193.1 0.2 fusion.9
  193.2 4.1 scatter_custom_fusion.1
  197.3 0.0 reduce-scatter.7.cloned.1.call-update
  197.4 0.0 reduce-scatter.9.cloned.1.call-start
  197.4 52.7 %reduce-scatter.7.cloned.1.call-done = f32[16,256]{1,0:T(8,128)} async-done(((f32[256,256]{1,0:T(8,128)}), f32[16,256]{1,0:T(8,128)}) %reduce-scatter.7.cloned.1.call-update) | async-done | bytes 16400 | tf_op jit(solution)/shard_map/reduce_scatter | solution.py:35
  250.1 1.3 multiply_reduce_fusion.3
  251.4 0.2 multiply_reduce_fusion.2
  251.6 0.1 multiply_add_fusion.2
  251.7 20.2 %all_gather.14 = f32[256,256]{1,0:T(8,128)S(1)} all-gather(f32[16,256]{1,0:T(8,128)S(1)} %multiply_add_fusion.2), channel_id=1, replica_groups=mesh['groups'=2,'builds'=16] {'builds'}, dimensions={0}, use_global_device_ids=true | all-gather | bytes 278528 | tf_op jit(solution)/shard_map/all_gather | solution.py:28
  271.9 1.6 gather_fusion.3
  273.4 0.2 fusion.11
  273.6 4.1 scatter_custom_fusion.2
  277.7 0.0 reduce-scatter.9.cloned.1.call-update
  277.7 0.0 reduce-scatter.11.cloned.1.call-start
  277.8 52.7 %reduce-scatter.9.cloned.1.call-done = f32[16,256]{1,0:T(8,128)} async-done(((f32[256,256]{1,0:T(8,128)}), f32[16,256]{1,0:T(8,128)}) %reduce-scatter.9.cloned.1.call-update) | async-done | bytes 16400 | tf_op jit(solution)/shard_map/reduce_scatter | solution.py:35
  330.4 0.0 copy-done
  330.5 1.1 multiply_reduce_fusion.1
  331.5 0.2 multiply_reduce_fusion
  331.7 0.1 multiply_add_fusion.1
  331.8 20.1 %all_gather.15 = f32[256,256]{1,0:T(8,128)S(1)} all-gather(f32[16,256]{1,0:T(8,128)S(1)} %multiply_add_fusion.1), channel_id=1, replica_groups=mesh['groups'=2,'builds'=16] {'builds'}, dimensions={0}, use_global_device_ids=true | all-gather | bytes 278528 | tf_op jit(solution)/shard_map/all_gather | solution.py:28
  351.9 1.6 gather_fusion.4
  353.5 0.2 fusion.13
  353.7 4.1 scatter_custom_fusion.3
  357.7 0.0 reduce-scatter.11.cloned.1.call-update
  357.8 52.7 %reduce-scatter.11.cloned.1.call-done = f32[16,256]{1,0:T(8,128)} async-done(((f32[256,256]{1,0:T(8,128)}), f32[16,256]{1,0:T(8,128)}) %reduce-scatter.11.cloned.1.call-update) | async-done | bytes 16400 | tf_op jit(solution)/shard_map/reduce_scatter | solution.py:35
  410.5 1.1 fusion.6
  411.5 0.7 multiply_add_fusion
  (13 shorter events, 0.1 us)
Async XLA Ops:
  6.5 12.5 %copy-start.3 = (s32[512]{0:T(512)S(1)}, s32[512]{0:T(512)}, u32[]{:S(2)}) copy-start(s32[512]{0:T(512)} %param.6) | copy-start | bytes 6148
  6.5 12.5 %copy-start.4 = (s32[512,1]{0,1:T(1,128)S(1)}, s32[512,1]{0,1:T(1,128)}, u32[]{:S(2)}) copy-start(s32[512,1]{0,1:T(1,128)} %param.7) | copy-start | bytes 6148
  6.5 20.3 %copy-start.1 = (f32[16,256]{1,0:T(8,128)S(1)}, f32[16,256]{1,0:T(8,128)}, u32[]{:S(2)}) copy-start(f32[16,256]{1,0:T(8,128)} %param.9) | copy-start | bytes 49156
  6.5 46.0 %copy-start.2 = (s32[512]{0:T(512)S(1)}, s32[512]{0:T(512)}, u32[]{:S(2)}) copy-start(s32[512]{0:T(512)} %param.8) | copy-start | bytes 6148
  6.5 104.1 %all-reduce.2.cloned.1.call-start = ((), (), s32[]{:S(2)}) async-start(), calls=%async_computation.5 | async-start | bytes 524288 | tf_op jit(solution)/shard_map/psum | solution.py:37
  19.0 151.0 %reduce-scatter.5.cloned.1.call-start = ((), (), s32[]{:S(2)}) async-start(), calls=%async_computation.4 | async-start | bytes 278528 | tf_op jit(solution)/shard_map/reduce_scatter | solution.py:35
  56.7 193.5 %reduce-scatter.7.cloned.1.call-start = ((), (), s32[]{:S(2)}) async-start(), calls=%async_computation.6 | async-start | bytes 278528 | tf_op jit(solution)/shard_map/reduce_scatter | solution.py:35
  110.7 219.8 %copy-start = (f32[256,256]{1,0:T(8,128)S(1)}, f32[256,256]{1,0:T(8,128)}, u32[]{:S(2)}) copy-start(f32[256,256]{1,0:T(8,128)} %all-reduce.2.cloned.1.call-done) | copy-start | bytes 786436
  197.4 133.1 %reduce-scatter.9.cloned.1.call-start = ((), (), s32[]{:S(2)}) async-start(), calls=%async_computation.7 | async-start | bytes 278528 | tf_op jit(solution)/shard_map/reduce_scatter | solution.py:35
  277.7 132.7 %reduce-scatter.11.cloned.1.call-start = ((), (), s32[]{:S(2)}) async-start(), calls=%async_computation.8 | async-start | bytes 278528 | tf_op jit(solution)/shard_map/reduce_scatter | solution.py:35
Sparse Core Ops, SparseCore 0:
  19.1 91.5 all-reduce.1
  114.2 55.7 reduce-scatter.4
  197.5 52.5 reduce-scatter.6
  277.9 52.5 reduce-scatter.8
  357.9 52.5 reduce-scatter.10
where the time goes:
time: 419 us
  waiting for transfers between devices  271 us (65%)
  blocking collectives  84.5 us (20%)
  other arithmetic  18.4 us (4%)
  matrix products  16.9 us (4%)
  local copies, waits for them, and re-layouts  14 us (3%)
  between operations  13.3 us (3%)
    reduce_scatter x4, waiting for transfers between devices, sparse_apply(): lax.psum_scatter(partial_value, 'builds', scatter_dimension=0, tiled=True)  217 us
    all_gather x4, blocking collectives, sparse_apply(): gathered = lax.all_gather(factors, 'builds', axis=0, tiled=True)  84.5 us
    psum x1, waiting for transfers between devices, shards(): shared = lax.psum(gram_local, 'builds')  53.9 us
    scatter-add x4, other arithmetic, sparse_apply(): jax.ops.segment_sum(coeffs[:, None] * wide_rows, test_ids, num_segments=t...  16.4 us
    dot_general x1, matrix products, shards(): lax.dot_general(build_factors, build_factors, (((0,), (0,)), ((), ())), p...  12.3 us
  transfers between devices with their start and end apart: 5, of which 5 were waited for; matrix products, arithmetic and copies ran while one was open for 3% of the time, Pallas kernels for 0%

commit v1 on v0

v1 whole, which is shorter than its diff:
```python
import functools

import jax
import jax.numpy as jnp
from jax import lax
from jax.experimental import pallas as pl
from jax.experimental.pallas import tpu as pltpu
from jax.sharding import PartitionSpec as P

ITERS = 3
MOST = 4
epsilon = 1e-06
f32 = jnp.float32
bf16 = jnp.bfloat16


def pieces(v):
    high = v.astype(bf16)
    rest = v - high.astype(f32)
    mid = rest.astype(bf16)
    low = (rest - mid.astype(f32)).astype(bf16)
    return jnp.concatenate([high, mid, low], axis=0)


def add_pieces(v):
    rows = v.shape[0] // 3
    return v[:rows] + v[rows : 2 * rows] + v[2 * rows :]


def nt(a, b):
    return lax.dot_general(a, b, (((1,), (1,)), ((), ())), preferred_element_type=f32)


def tn(a, b):
    return lax.dot_general(a, b, (((0,), (0,)), ((), ())), preferred_element_type=f32)


def kernel(
    n, owners, conf_scale, damping,
    x_hbm, picked, slot, count, start, out,
    x_buf, gram, tri, tri_in, tri_sum, y_out, y_in, w_out, w_in,
    x_sem, y_send, y_recv, w_send, w_recv, g_send, g_recv, s_send, s_recv,
):
    me = lax.axis_index("builds")
    chunks, chunk, _ = x_buf.shape
    tests = start.shape[0]
    slots = tests * MOST
    width = w_out.shape[2]
    part = tri.shape[1]
    half = tri.shape[2]

    def load(c):
        return pltpu.make_async_copy(
            x_hbm.at[pl.ds(pl.multiple_of(c * chunk, chunk), chunk), :], x_buf.at[c], x_sem.at[c]
        )

    @pl.loop(0, chunks)
    def _(c):
        load(c).start()

    barrier = pltpu.get_barrier_semaphore()

    @pl.loop(1, n)
    def _(j):
        pl.semaphore_signal(
            barrier, inc=1, device_id={"builds": lax.rem(me + j, n)}, device_id_type=pl.DeviceIdType.MESH
        )

    def remote(src, dst, send, recv, to):
        return pltpu.make_async_remote_copy(
            src_ref=src, dst_ref=dst, send_sem=send, recv_sem=recv,
            device_id={"builds": to}, device_id_type=pl.DeviceIdType.MESH,
        )

    def y_copy(to, source):
        return remote(y_out.at[to], y_in.at[source], y_send.at[to], y_recv.at[source], to)

    def w_copy(to, source):
        return remote(w_out.at[to], w_in.at[source], w_send.at[to], w_recv.at[source], to)

    def block_of(owner):
        local = slot[...] - owner * slots
        local = jnp.where((local >= 0) & (local < slots), local, -1)
        row = lax.broadcasted_iota(jnp.int32, (width, local.shape[1]), 0)
        place = (row == local).astype(f32).astype(bf16)
        rows = jnp.dot(place[:slots], picked[...], preferred_element_type=f32).astype(bf16)
        counts = nt(count[...], place)
        test = lax.broadcasted_iota(jnp.int32, counts.shape, 0)
        lane = lax.broadcasted_iota(jnp.int32, counts.shape, 1)
        return rows, jnp.where(lane // MOST == test, counts, 0.0).astype(bf16)

    rows, counts = block_of(me)
    y_in[me] = rows
    w_in[me] = counts
    pl.semaphore_wait(barrier, n - 1)

    @pl.loop(1, n)
    def _(j):
        to = lax.rem(me + j, n)
        rows, counts = block_of(to)
        y_out[to] = rows
        w_out[to] = counts
        y_copy(to, me).start()
        w_copy(to, me).start()

    gram[...] = jnp.zeros_like(gram)

    @pl.loop(0, chunks)
    def _(c):
        load(c).wait()
        x = x_buf[c]
        gram[...] += tn(x, x)

    per = half // part
    for i in range(per):
        tri[i] = gram[i * part : (i + 1) * part, :half]
        tri[per + i] = gram[i * part : (i + 1) * part, half:]
        tri[2 * per + i] = gram[half + i * part : half + (i + 1) * part, half:]

    share = tri.shape[0] // owners

    def g_copy(to, source):
        return remote(
            tri.at[pl.ds(to * share, share)], tri_in.at[source], g_send.at[to], g_recv.at[source], to
        )

    def s_copy(to, source):
        tiles = pl.ds(source * share, share)
        return remote(tri_sum.at[tiles], tri_sum.at[tiles], s_send.at[to], s_recv.at[source], to)

    def each_owner(body):
        @pl.loop(1, n)
        def _(j):
            other = lax.rem(me + j, n)
            if owners == n:
                body(other)
            else:
                pl.when(other < owners)(lambda: body(other))

    def each_other(body):
        @pl.loop(1, n)
        def _(j):
            body(lax.rem(me + j, n))

    def if_owner(body):
        if owners == n:
            body()
        else:
            pl.when(me < owners)(body)

    each_owner(lambda to: g_copy(to, me).start())

    def reduce():
        tri_in[me] = tri[pl.ds(me * share, share)]
        each_other(lambda source: g_copy(me, source).wait_recv())
        tri_sum[pl.ds(me * share, share)] = jnp.sum(tri_in[...], axis=0)
        each_other(lambda to: s_copy(to, me).start())

    if_owner(reduce)

    def finish_y(source):
        y_copy(source, source).wait_recv()
        w_copy(source, source).wait_recv()

    each_other(finish_y)

    groups = []
    for d in range(0, n, 2):
        groups.append(w_in[d].astype(f32) + pltpu.roll(w_in[d + 1].astype(f32), slots, 1))
    weight = jnp.concatenate(groups, axis=1) * conf_scale
    ys = y_in[...].reshape(n * slots, y_in.shape[2])

    def sparse(v3, target):
        inner = add_pieces(nt(v3, ys))
        coeffs = weight * (1.0 - inner) if target else weight * inner
        return add_pieces(jnp.dot(pieces(coeffs), ys, preferred_element_type=f32))

    factors = start[...]
    v3 = pieces(factors)
    residual = sparse(v3, True)

    each_owner(lambda source: s_copy(source, source).wait_recv())
    per_rows = tri_sum[...].reshape(3 * half, half)
    cross = per_rows[half : 2 * half]
    shared = jnp.concatenate(
        [
            jnp.concatenate([per_rows[:half], cross], axis=1),
            jnp.concatenate([cross.T, per_rows[2 * half :]], axis=1),
        ],
        axis=0,
    )
    shared3 = pieces(shared)

    def dense(v, v3):
        wide = add_pieces(nt(v3, shared3))
        rank = v.shape[1]
        return wide[:, :rank] + wide[:, rank : 2 * rank] + wide[:, 2 * rank :] + damping * v

    residual = residual - dense(factors, v3)
    direction = residual
    norm_now = jnp.sum(residual * residual, axis=1, keepdims=True)
    for sweep in range(ITERS):
        v3 = pieces(direction)
        image = sparse(v3, False) + dense(direction, v3)
        step = norm_now / (jnp.sum(direction * image, axis=1, keepdims=True) + epsilon)
        factors = factors + step * direction
        if sweep + 1 < ITERS:
            residual = residual - step * image
            norm_next = jnp.sum(residual * residual, axis=1, keepdims=True)
            direction = residual + (norm_next / (norm_now + epsilon)) * direction
            norm_now = norm_next
    out[...] = factors

    def sent(to):
        y_copy(to, me).wait_send()
        w_copy(to, me).wait_send()

    each_other(sent)
    each_owner(lambda to: g_copy(to, me).wait_send())
    if_owner(lambda: each_other(lambda to: s_copy(to, me).wait_send()))


def shards(build_factors, nz_build, nz_test, nz_count, start_factors):
    tests, rank = start_factors.shape
    bld_rows = build_factors.shape[0]
    nz_rows = nz_build.shape[0]
    n = lax.axis_size("builds")
    conf_scale = n * bld_rows * tests / (8.0 * nz_rows)
    damping = 0.4 * conf_scale
    ids = nz_test[:, 0]
    number = jnp.arange(nz_rows, dtype=jnp.int32)
    earlier = (ids[:, None] == ids[None, :]) & (number[:, None] < number[None, :])
    slot = (ids * MOST + jnp.sum(earlier, axis=0, dtype=jnp.int32))[None, :]
    count = jnp.broadcast_to(nz_count.astype(bf16)[None, :], (tests, nz_rows))
    picked = build_factors[nz_build]

    slots = tests * MOST
    half = rank // 2
    part = 8
    tiles = 3 * half // part
    owners = max(k for k in range(1, min(n, tiles) + 1) if tiles % k == 0)
    share = tiles // owners
    chunk = 2048
    chunks = bld_rows // chunk
    vmem = pl.BlockSpec(memory_space=pltpu.VMEM)
    dma = pltpu.SemaphoreType.DMA
    return pl.pallas_call(
        functools.partial(kernel, n, owners, conf_scale, damping),
        out_shape=jax.ShapeDtypeStruct((tests, rank), f32),
        in_specs=[pl.BlockSpec(memory_space=pl.ANY)] + [vmem] * 4,
        out_specs=vmem,
        scratch_shapes=[
            pltpu.VMEM((chunks, chunk, rank), bf16),
            pltpu.VMEM((rank, rank), f32),
            pltpu.VMEM((tiles, part, half), f32),
            pltpu.VMEM((n, share, part, half), f32),
            pltpu.VMEM((tiles, part, half), f32),
            pltpu.VMEM((n, slots, rank), bf16),
            pltpu.VMEM((n, slots, rank), bf16),
            pltpu.VMEM((n, tests, 128), bf16),
            pltpu.VMEM((n, tests, 128), bf16),
            dma((chunks,)),
        ]
        + [dma((n,))] * 8,
        compiler_params=pltpu.CompilerParams(
            collective_id=0, has_side_effects=True, vmem_limit_bytes=48 * 1024 * 1024
        ),
    )(build_factors, picked, slot, count, start_factors)


def solution(mesh):
    return jax.shard_map(
        shards,
        mesh=mesh,
        in_specs=(
            P("builds", None),
            P(("groups", "builds")),
            P(("groups", "builds"), None),
            P(("groups", "builds")),
            P(("groups", "builds"), None),
        ),
        out_specs=P(("groups", "builds"), None),
        check_vma=False,
    )
```

time: 419 us -> 47 us (0.11)
  waiting for transfers between devices: 271 us -> 0 us
  blocking collectives: 84.5 us -> 0 us
  Pallas kernels: 0 us -> 34.6 us
  matrix products: 16.9 us -> 0 us
  other arithmetic: 18.4 us -> 2.99 us
  between operations: 13.3 us -> 0.03 us
  local copies, waits for them, and re-layouts: 14 us -> 9.08 us
    reduce_scatter x4 -> x0, waiting for transfers between devices: 217 us -> none  [sparse_apply(): lax.psum_scatter(partial_value, 'builds', scatter_dimension=0, tiled=True)]
    all_gather x4 -> x0, blocking collectives: 84.5 us -> none  [sparse_apply(): gathered = lax.all_gather(factors, 'builds', axis=0, tiled=True)]
    psum x1 -> x0, waiting for transfers between devices: 53.9 us -> none  [shards(): shared = lax.psum(gram_local, 'builds')]
    pallas_call x0 -> x1, Pallas kernels: none -> 34.6 us  [shards(): pl.pallas_call(functools.partial(kernel, n, owners, conf_scale, damping),...]
    dot_general x5 -> x0, matrix products: 16.9 us -> none  [the longest x1 12.3 us: shards(): lax.dot_general(build_factors, build_factors, (((0,), (0,)), ((), ())), p...]
    scatter-add x4 -> x0, other arithmetic: 16.4 us -> none  [sparse_apply(): jax.ops.segment_sum(coeffs[:, None] * wide_rows, test_ids, num_segments=t...]
    gather x5 -> x1, local copies, waits for them, and re-layouts: 14 us -> 7.75 us  [shards(): picked = build_factors[nz_build]]
  transfers between devices with their start and end apart: 5 -> 0, of which waited for: 5 -> 0; matrix products, arithmetic and copies ran while one was open for 3% -> 0% of each run, Pallas kernels for 0% -> 0%
where the time goes in v1:
time: 47 us; the launch traced here: 46.7 us
  Pallas kernels  34.6 us (74%)
  local copies, waits for them, and re-layouts  9.08 us (19%)
  other arithmetic  2.99 us (6%)
    pallas_call x1, Pallas kernels, shards(): pl.pallas_call(functools.partial(kernel, n, owners, conf_scale, damping),...  34.6 us
    gather x1, local copies, waits for them, and re-layouts, shards(): picked = build_factors[nz_build]  7.75 us
    unnamed x3, local copies, waits for them, and re-layouts  1.32 us

profile of v1, /device:TPU:0, one launch (start us, length us, event | category | flops | bytes accessed | tf_op | source)
XLA Modules:
  0.0 46.7 jit_solution(10982002282867624138)
XLA Ops:
  0.0 0.7 %convert_element_type.7 = bf16[512]{0:T(512)(128)(2,1)S(1)} convert(s32[512]{0:T(512)} %param.8) | non-fusion elementwise | flops 512 | bytes 3072 | tf_op jit(solution)/shard_map/convert_element_type | solution.py:234
  0.7 0.7 %compare_select_fusion = s32[512]{0:T(512)S(1)} fusion(s32[512]{0:T(512)} %param.6), kind=kLoop, calls=%fused_computation.4 | loop fusion | flops 1536 | bytes 4096 | tf_op jit(solution)/shard_map/select_n | solution.py:235
  1.4 0.9 %convert_reduce_fusion = s32[512]{0:T(512)S(1)} fusion(s32[512]{0:T(512)} %bitcast.4), kind=kLoop, calls=%fused_computation.1 | loop fusion | flops 1310208 | bytes 4096 | tf_op jit(solution)/shard_map/reduce_sum | solution.py:233
  2.3 0.7 %bitcast_add_fusion.slot = s32[1,512]{1,0:T(1,128)S(1)} fusion(s32[1,512]{1,0:T(1,128)S(1)} %bitcast.5, s32[512,1]{0,1:T(1,128)} %param.7), kind=kLoop, calls=%fused_computation.6 | loop fusion | flops 1024 | bytes 6144 | tf_op jit(solution)/shard_map/add | solution.py:233
  3.0 7.8 %gather_fusion = bf16[512,256]{1,0:T(8,128)(2,1)S(1)} fusion(bf16[24576,256]{1,0:T(8,128)(2,1)} %x_hbm.1, s32[1024]{0:T(1024)S(1)} %pad_clamp_fusion), kind=kCustom, calls=%fused_computation | custom fusion | bytes 526336 | tf_op jit(solution)/shard_map/gather | solution.py:235
  10.8 0.0 copy-start
  10.8 0.7 %copy-done = f32[16,256]{1,0:T(8,128)S(1)} copy-done((f32[16,256]{1,0:T(8,128)S(1)}, f32[16,256]{1,0:T(8,128)}, u32[]{:S(2)}) %copy-start) | copy-done | bytes 16408
  11.5 34.6 %shard_map.55 = f32[16,256]{1,0:T(8,128)S(1)} custom-call(bf16[24576,256]{1,0:T(8,128)(2,1)} %x_hbm.1, bf16[512,256]{1,0:T(8,128)(2,1)S(1)} %gather_fusion, s32[1,512]{1,0:T(1,128)S(1)} %bitcast_add_fusion.slot, bf16[16,512]{1,0:T(8,128)(2,1)S(1)} %broadcast_in_dim.5.count, f32[16,256]{1,0:T(8,128)S(1)} %copy-done), custom_call_target="tpu_custom_call" | custom-call | tf_op jit(solution)/shard_map/pallas_call | solution.py:247
  46.1 0.6 %copy.7 = f32[16,256]{1,0:T(8,128)} copy(f32[16,256]{1,0:T(8,128)S(1)} %shard_map.55) | data formatting | bytes 32768
  (2 shorter events, 0.0 us)
Async XLA Ops:
  10.8 0.7 %copy-start = (f32[16,256]{1,0:T(8,128)S(1)}, f32[16,256]{1,0:T(8,128)}, u32[]{:S(2)}) copy-start(f32[16,256]{1,0:T(8,128)} %start.1) | copy-start | bytes 49156

commit v2 on v1

--- a/solution.py
+++ b/solution.py
@@ -37,12 +37,15 @@
 
 def kernel(
     n, owners, conf_scale, damping,
-    x_hbm, picked, slot, count, start, out,
-    x_buf, gram, tri, tri_in, tri_sum, y_out, y_in, w_out, w_in,
+    nz_at, x_hbm, nz_row, test_row, count_row, start, out,
+    x_buf, picked, slot, select, gram, tri, tri_in, tri_sum, y_out, y_in, w_out, w_in,
     x_sem, y_send, y_recv, w_send, w_recv, g_send, g_recv, s_send, s_recv,
 ):
     me = lax.axis_index("builds")
-    chunks, chunk, _ = x_buf.shape
+    chunks = x_sem.shape[0]
+    lumps, lump, rank = x_buf.shape
+    chunk = lumps // chunks
+    nz = slot.shape[1]
     tests = start.shape[0]
     slots = tests * MOST
     width = w_out.shape[2]
@@ -51,7 +54,7 @@
 
     def load(c):
         return pltpu.make_async_copy(
-            x_hbm.at[pl.ds(pl.multiple_of(c * chunk, chunk), chunk), :], x_buf.at[c], x_sem.at[c]
+            x_hbm.at[pl.ds(c * chunk, chunk)], x_buf.at[pl.ds(c * chunk, chunk)], x_sem.at[c]
         )
 
     @pl.loop(0, chunks)
@@ -65,6 +68,24 @@
         pl.semaphore_signal(
             barrier, inc=1, device_id={"builds": lax.rem(me + j, n)}, device_id_type=pl.DeviceIdType.MESH
         )
+
+    tests_at = jnp.broadcast_to(test_row[...].astype(f32), (128, nz)).T
+
+    @pl.loop(0, nz // 128)
+    def _(c):
+        lanes = pl.ds(pl.multiple_of(c * 128, 128), 128)
+        ids = test_row[:, lanes]
+        first = lax.broadcasted_iota(jnp.int32, (nz, 128), 0)
+        second = lax.broadcasted_iota(jnp.int32, (nz, 128), 1) + c * 128
+        same = (tests_at == ids.astype(f32)) & (first < second)
+        earlier = jnp.sum(same.astype(f32), axis=0, keepdims=True)
+        slot[:, lanes] = ids * MOST + earlier.astype(jnp.int32)
+
+    number = lax.broadcasted_iota(jnp.int32, (1, nz), 1)
+    place = (number % lump) * lump + nz_row[...] % lump
+    column = lax.broadcasted_iota(jnp.int32, (lump * lump, nz), 0)
+    select[...] = (column == place).astype(f32).T.astype(bf16)
+    count = jnp.broadcast_to(count_row[...].astype(f32), (tests, nz)).astype(bf16)
 
     def remote(src, dst, send, recv, to):
         return pltpu.make_async_remote_copy(
@@ -84,15 +105,68 @@
         row = lax.broadcasted_iota(jnp.int32, (width, local.shape[1]), 0)
         place = (row == local).astype(f32).astype(bf16)
         rows = jnp.dot(place[:slots], picked[...], preferred_element_type=f32).astype(bf16)
-        counts = nt(count[...], place)
+        counts = nt(count, place)
         test = lax.broadcasted_iota(jnp.int32, counts.shape, 0)
         lane = lax.broadcasted_iota(jnp.int32, counts.shape, 1)
         return rows, jnp.where(lane // MOST == test, counts, 0.0).astype(bf16)
 
+    gram[...] = jnp.zeros_like(gram)
+
+    @pl.loop(0, chunks)
+    def _(c):
+        load(c).wait()
+        x = x_buf[pl.ds(c * chunk, chunk)].reshape(chunk * lump, rank)
+        gram[...] += tn(x, x)
+
+    per = half // part
+    for i in range(per):
+        tri[i] = gram[i * part : (i + 1) * part, :half]
+        tri[per + i] = gram[i * part : (i + 1) * part, half:]
+        tri[2 * per + i] = gram[half + i * part : half + (i + 1) * part, half:]
+
+    share = tri.shape[0] // owners
+
+    def g_copy(to, source):
+        return remote(
+            tri.at[pl.ds(to * share, share)], tri_in.at[source], g_send.at[to], g_recv.at[source], to
+        )
+
+    def s_copy(to, source):
+        tiles = pl.ds(source * share, share)
+        return remote(tri_sum.at[tiles], tri_sum.at[tiles], s_send.at[to], s_recv.at[source], to)
+
+    def each_owner(body):
+        @pl.loop(1, n)
+        def _(j):
+            other = lax.rem(me + j, n)
+            if owners == n:
+                body(other)
+            else:
+                pl.when(other < owners)(lambda: body(other))
+
+    def each_other(body):
+        @pl.loop(1, n)
+        def _(j):
+            body(lax.rem(me + j, n))
+
+    def if_owner(body):
+        if owners == n:
+            body()
+        else:
+            pl.when(me < owners)(body)
+
+    pl.semaphore_wait(barrier, n - 1)
+    each_owner(lambda to: g_copy(to, me).start())
+
+    @pl.loop(0, nz // lump)
+    def _(b):
+        near = jnp.concatenate([x_buf[nz_at[b * lump + i] // lump] for i in range(lump)], axis=0)
+        rows = pl.ds(pl.multiple_of(b * lump, lump), lump)
+        picked[rows, :] = jnp.dot(select[rows, :], near, preferred_element_type=f32).astype(bf16)
+
     rows, counts = block_of(me)
     y_in[me] = rows
     w_in[me] = counts
-    pl.semaphore_wait(barrier, n - 1)
 
     @pl.loop(1, n)
     def _(j):
@@ -103,52 +177,6 @@
         y_copy(to, me).start()
         w_copy(to, me).start()
 
-    gram[...] = jnp.zeros_like(gram)
-
-    @pl.loop(0, chunks)
-    def _(c):
-        load(c).wait()
-        x = x_buf[c]
-        gram[...] += tn(x, x)
-
-    per = half // part
-    for i in range(per):
-        tri[i] = gram[i * part : (i + 1) * part, :half]
-        tri[per + i] = gram[i * part : (i + 1) * part, half:]
-        tri[2 * per + i] = gram[half + i * part : half + (i + 1) * part, half:]
-
-    share = tri.shape[0] // owners
-
-    def g_copy(to, source):
-        return remote(
-            tri.at[pl.ds(to * share, share)], tri_in.at[source], g_send.at[to], g_recv.at[source], to
-        )
-
-    def s_copy(to, source):
-        tiles = pl.ds(source * share, share)
-        return remote(tri_sum.at[tiles], tri_sum.at[tiles], s_send.at[to], s_recv.at[source], to)
-
-    def each_owner(body):
-        @pl.loop(1, n)
-        def _(j):
-            other = lax.rem(me + j, n)
-            if owners == n:
-                body(other)
-            else:
-                pl.when(other < owners)(lambda: body(other))
-
-    def each_other(body):
-        @pl.loop(1, n)
-        def _(j):
-            body(lax.rem(me + j, n))
-
-    def if_owner(body):
-        if owners == n:
-            body()
-        else:
-            pl.when(me < owners)(body)
-
-    each_owner(lambda to: g_copy(to, me).start())
 
     def reduce():
         tri_in[me] = tri[pl.ds(me * share, share)]
@@ -227,30 +255,26 @@
     n = lax.axis_size("builds")
     conf_scale = n * bld_rows * tests / (8.0 * nz_rows)
     damping = 0.4 * conf_scale
-    ids = nz_test[:, 0]
-    number = jnp.arange(nz_rows, dtype=jnp.int32)
-    earlier = (ids[:, None] == ids[None, :]) & (number[:, None] < number[None, :])
-    slot = (ids * MOST + jnp.sum(earlier, axis=0, dtype=jnp.int32))[None, :]
-    count = jnp.broadcast_to(nz_count.astype(bf16)[None, :], (tests, nz_rows))
-    picked = build_factors[nz_build]
-
     slots = tests * MOST
     half = rank // 2
     part = 8
     tiles = 3 * half // part
     owners = max(k for k in range(1, min(n, tiles) + 1) if tiles % k == 0)
     share = tiles // owners
-    chunk = 2048
-    chunks = bld_rows // chunk
+    lump = 16
+    chunks = bld_rows // 2048
     vmem = pl.BlockSpec(memory_space=pltpu.VMEM)
     dma = pltpu.SemaphoreType.DMA
     return pl.pallas_call(
         functools.partial(kernel, n, owners, conf_scale, damping),
         out_shape=jax.ShapeDtypeStruct((tests, rank), f32),
-        in_specs=[pl.BlockSpec(memory_space=pl.ANY)] + [vmem] * 4,
+        in_specs=[pl.BlockSpec(memory_space=pltpu.SMEM), pl.BlockSpec(memory_space=pl.ANY)] + [vmem] * 4,
         out_specs=vmem,
         scratch_shapes=[
-            pltpu.VMEM((chunks, chunk, rank), bf16),
+            pltpu.VMEM((bld_rows // lump, lump, rank), bf16),
+            pltpu.VMEM((nz_rows, rank), bf16),
+            pltpu.VMEM((1, nz_rows), jnp.int32),
+            pltpu.VMEM((nz_rows, lump * lump), bf16),
             pltpu.VMEM((rank, rank), f32),
             pltpu.VMEM((tiles, part, half), f32),
             pltpu.VMEM((n, share, part, half), f32),
@@ -265,7 +289,14 @@
         compiler_params=pltpu.CompilerParams(
             collective_id=0, has_side_effects=True, vmem_limit_bytes=48 * 1024 * 1024
         ),
-    )(build_factors, picked, slot, count, start_factors)
+    )(
+        nz_build,
+        build_factors.reshape(bld_rows // lump, lump, rank),
+        nz_build[None, :],
+        nz_test.reshape(1, nz_rows),
+        nz_count[None, :],
+        start_factors,
+    )
 
 
 def solution(mesh):

time: 47 us -> 44.1 us (0.938)
  Pallas kernels: 34.6 us -> 40.4 us
  local copies, waits for them, and re-layouts: 9.08 us -> 3.37 us
  other arithmetic: 2.99 us -> 0 us
    gather x1 -> x0, local copies, waits for them, and re-layouts: 7.75 us -> none  [shards(): picked = build_factors[nz_build]]
    pallas_call x1, Pallas kernels: 34.6 us -> 40.4 us  [shards(): pl.pallas_call(functools.partial(kernel, n, owners, conf_scale, damping),...]
    unnamed x3 -> x9, local copies, waits for them, and re-layouts: 1.32 us -> 3.37 us
    reduce_sum x1 -> x0, other arithmetic: 0.92 us -> none  [shards(): slot = (ids * MOST + jnp.sum(earlier, axis=0, dtype=jnp.int32))[None, :]]
    add x1 -> x0, other arithmetic: 0.69 us -> none  [shards(): slot = (ids * MOST + jnp.sum(earlier, axis=0, dtype=jnp.int32))[None, :]]
    convert_element_type x1 -> x0, other arithmetic: 0.68 us -> none  [shards(): count = jnp.broadcast_to(nz_count.astype(bf16)[None, :], (tests, nz_rows))]
    select_n x1 -> x0, other arithmetic: 0.68 us -> none  [shards(): picked = build_factors[nz_build]]
where the time goes in v2:
time: 44.1 us; the launch traced here: 43.8 us
  Pallas kernels  40.4 us (92%)
  local copies, waits for them, and re-layouts  3.37 us (8%)
    pallas_call x1, Pallas kernels, shards(): pl.pallas_call(functools.partial(kernel, n, owners, conf_scale, damping),...  40.4 us
    unnamed x9, local copies, waits for them, and re-layouts  3.37 us

profile of v2, /device:TPU:0, one launch (start us, length us, event | category | flops | bytes accessed | tf_op | source)
XLA Modules:
  0.0 43.8 jit_solution(6782998905289734265)
XLA Ops:
  0.0 0.0 copy-start
  0.0 0.7 %copy-done = f32[16,256]{1,0:T(8,128)S(1)} copy-done((f32[16,256]{1,0:T(8,128)S(1)}, f32[16,256]{1,0:T(8,128)}, u32[]{:S(2)}) %copy-start) | copy-done | bytes 16408
  0.7 0.0 copy-start.1
  0.7 0.7 %copy-done.1 = s32[512]{0:T(512)S(1)} copy-done((s32[512]{0:T(512)S(1)}, s32[512]{0:T(512)}, u32[]{:S(2)}) %copy-start.1) | copy-done | bytes 2072
  1.4 0.0 copy-start.2
  1.4 0.7 %copy-done.2 = s32[512,1]{0,1:T(1,128)S(1)} copy-done((s32[512,1]{0,1:T(1,128)S(1)}, s32[512,1]{0,1:T(1,128)}, u32[]{:S(2)}) %copy-start.2) | copy-done | bytes 2072
  2.1 0.0 copy-start.3
  2.1 0.7 %copy-done.3 = s32[512]{0:T(512)S(1)} copy-done((s32[512]{0:T(512)S(1)}, s32[512]{0:T(512)}, u32[]{:S(2)}) %copy-start.3) | copy-done | bytes 2072
  2.8 40.4 %shard_map.55 = f32[16,256]{1,0:T(8,128)S(1)} custom-call(s32[512]{0:T(512)S(1)} %copy-done.1, bf16[1536,16,256]{2,1,0:T(8,128)(2,1)} %bitcast.7, s32[1,512]{1,0:T(1,128)S(1)} %bitcast.4, s32[1,512]{1,0:T(1,128)S(1)} %bitcast.5, s32[1,512]{1,0:T(1,128)S(1)} %bitcast.6, f32[16,256]{1,0:T(8,128)S(1)} %copy-done), custom_call_target="tpu_custom_call" | custom-call | tf_op jit(solution)/shard_map/pallas_call | solution.py:268
  43.2 0.6 %copy.7 = f32[16,256]{1,0:T(8,128)} copy(f32[16,256]{1,0:T(8,128)S(1)} %shard_map.55) | data formatting | bytes 32768
Async XLA Ops:
  0.0 0.7 %copy-start = (f32[16,256]{1,0:T(8,128)S(1)}, f32[16,256]{1,0:T(8,128)}, u32[]{:S(2)}) copy-start(f32[16,256]{1,0:T(8,128)} %start.1) | copy-start | bytes 49156
  0.7 0.7 %copy-start.1 = (s32[512]{0:T(512)S(1)}, s32[512]{0:T(512)}, u32[]{:S(2)}) copy-start(s32[512]{0:T(512)} %nz_at.1) | copy-start | bytes 6148
  1.4 0.7 %copy-start.2 = (s32[512,1]{0,1:T(1,128)S(1)}, s32[512,1]{0,1:T(1,128)}, u32[]{:S(2)}) copy-start(s32[512,1]{0,1:T(1,128)} %param.7) | copy-start | bytes 6148
  2.1 0.7 %copy-start.3 = (s32[512]{0:T(512)S(1)}, s32[512]{0:T(512)}, u32[]{:S(2)}) copy-start(s32[512]{0:T(512)} %param.8) | copy-start | bytes 6148

commit v3 on v2

v3 whole, which is shorter than its diff:
```python
import functools

import jax
import jax.numpy as jnp
from jax import lax
from jax.experimental import pallas as pl
from jax.experimental.pallas import tpu as pltpu
from jax.sharding import PartitionSpec as P

ITERS = 3
MOST = 4
PLANE = 4
epsilon = 1e-06
f32 = jnp.float32
bf16 = jnp.bfloat16


def pieces(v):
    high = v.astype(bf16)
    rest = v - high.astype(f32)
    mid = rest.astype(bf16)
    low = (rest - mid.astype(f32)).astype(bf16)
    return jnp.concatenate([high, mid, low], axis=0)


def add_pieces(v):
    rows = v.shape[0] // 3
    return v[:rows] + v[rows : 2 * rows] + v[2 * rows :]


def nt(a, b):
    return lax.dot_general(a, b, (((1,), (1,)), ((), ())), preferred_element_type=f32)


def tn(a, b):
    return lax.dot_general(a, b, (((0,), (0,)), ((), ())), preferred_element_type=f32)


def kernel(
    n, owners, conf_scale, damping,
    nz_hbm, test_hbm, count_hbm, start_hbm, x_hbm, out,
    nz_row, test_row, count_row, start, x_buf, slot, packed, counts_at, at_vmem, at, select, gram,
    tri, plane_in, plane_sum, line_in, tri_sum, y_out, y_in, w_out, w_in,
    x_sem, in_sem, y_send, y_recv, w_send, w_recv,
    a_send, a_recv, b_send, b_recv, c_send, c_recv, d_send, d_recv,
):
    me = lax.axis_index("builds")
    chunks = x_sem.shape[0]
    lumps, lump, rank = x_buf.shape
    chunk = lumps // chunks
    nz = slot.shape[1]
    tests = start.shape[0]
    slots = tests * MOST
    part = tri.shape[1]
    half = tri.shape[2]
    tiles = tri.shape[0]
    line = n // PLANE
    z, p = me // PLANE, lax.rem(me, PLANE)

    small = [
        pltpu.make_async_copy(src, dst, in_sem.at[i])
        for i, (src, dst) in enumerate(
            [(nz_hbm, nz_row), (test_hbm, test_row), (count_hbm, count_row), (start_hbm, start)]
        )
    ]
    for copy in small:
        copy.start()

    def load(c):
        return pltpu.make_async_copy(
            x_hbm.at[pl.ds(c * chunk, chunk)], x_buf.at[pl.ds(c * chunk, chunk)], x_sem.at[c]
        )

    @pl.loop(0, chunks)
    def _(c):
        load(c).start()

    barrier = pltpu.get_barrier_semaphore()

    @pl.loop(1, n)
    def _(j):
        pl.semaphore_signal(
            barrier, inc=1, device_id={"builds": lax.rem(me + j, n)}, device_id_type=pl.DeviceIdType.MESH
        )

    for copy in small:
        copy.wait()

    tests_at = jnp.broadcast_to(test_row[...], (128, nz)).T

    @pl.loop(0, nz // 128)
    def _(c):
        lanes = pl.ds(pl.multiple_of(c * 128, 128), 128)
        ids = test_row[:, lanes]
        first = lax.broadcasted_iota(jnp.int32, (nz, 128), 0)
        second = lax.broadcasted_iota(jnp.int32, (nz, 128), 1) + c * 128
        same = (tests_at == ids) & (first < second)
        earlier = jnp.sum(same.astype(jnp.int32), axis=0, keepdims=True)
        slot[:, lanes] = ids * MOST + earlier

    slot_at = jnp.broadcast_to(slot[...], (128, nz)).T
    packed[...] = jnp.broadcast_to(nz_row[...] * 16 + count_row[...], (128, nz)).T

    @pl.loop(0, n * slots // 128)
    def _(c):
        lane = lax.broadcasted_iota(jnp.int32, (1, 128), 1)
        wanted = lane + c * 128
        held = jnp.sum(jnp.where(slot_at == wanted, packed[...], 0), axis=0, keepdims=True)
        row, amount = held // 16, held % 16
        at_vmem[pl.ds(c, 1), :] = jnp.clip(row // lump, 0, lumps - 1)
        counts_at[pl.ds(c, 1), :] = amount.astype(f32)
        place = jnp.where(amount > 0, (lane % lump) * lump + row % lump, -1)
        place = jnp.broadcast_to(place.astype(f32), (128, 128)).T
        column = lax.broadcasted_iota(jnp.int32, (128, 128), 1).astype(f32)
        both = [(place == column + h * 128.0).astype(f32) for h in range(lump * lump // 128)]
        select[pl.ds(pl.multiple_of(c * 128, 128), 128), :] = jnp.concatenate(both, axis=1).astype(bf16)

    to_scalars = pltpu.make_async_copy(at_vmem, at, in_sem.at[0])
    to_scalars.start()

    def remote(src, dst, send, recv, to):
        return pltpu.make_async_remote_copy(
            src_ref=src, dst_ref=dst, send_sem=send, recv_sem=recv,
            device_id={"builds": to}, device_id_type=pl.DeviceIdType.MESH,
        )

    def y_copy(to, source):
        return remote(y_out.at[to], y_in.at[source], y_send.at[to], y_recv.at[source], to)

    def w_copy(to, source):
        return remote(w_out.at[to], w_in.at[source], w_send.at[to], w_recv.at[source], to)

    pair = 128 // slots

    def block_of(owner):
        line_at, lane_at = owner // pair, lax.rem(owner, pair) * slots
        rows = []
        for b in range(slots // lump):
            near = jnp.concatenate(
                [x_buf[at[line_at, lane_at + b * lump + i]] for i in range(lump)], axis=0
            )
            chosen = select[pl.ds(pl.multiple_of(owner * slots + b * lump, lump), lump), :]
            rows.append(jnp.dot(chosen, near, preferred_element_type=f32).astype(bf16))
        counts = jnp.broadcast_to(counts_at[pl.ds(line_at, 1), :], (tests, 128))
        counts = pltpu.roll(counts, lax.rem(128 - lane_at, 128), 1)
        test = lax.broadcasted_iota(jnp.int32, counts.shape, 0)
        lane = lax.broadcasted_iota(jnp.int32, counts.shape, 1)
        return jnp.concatenate(rows, axis=0), jnp.where(lane // MOST == test, counts, 0.0).astype(bf16)

    gram[...] = jnp.zeros_like(gram)

    @pl.loop(0, chunks)
    def _(c):
        load(c).wait()
        x = x_buf[pl.ds(c * chunk, chunk)].reshape(chunk * lump, rank)
        gram[...] += tn(x, x)

    per = half // part
    for i in range(per):
        tri[i] = gram[i * part : (i + 1) * part, :half]
        tri[per + i] = gram[i * part : (i + 1) * part, half:]
        tri[2 * per + i] = gram[half + i * part : half + (i + 1) * part, half:]

    quarter = tiles // PLANE
    share = quarter // owners

    def in_plane(body):
        for k in range(1, PLANE):
            body(lax.rem(p + k, PLANE))

    def in_line(body, only_owners=False):
        @pl.loop(1, line)
        def _(k):
            other = lax.rem(z + k, line)
            if only_owners and owners < line:
                pl.when(other < owners)(lambda: body(other))
            else:
                body(other)

    def if_owner(body):
        if owners == line:
            body()
        else:
            pl.when(z < owners)(body)

    def a_copy(to, source):
        return remote(
            tri.at[pl.ds(to * quarter, quarter)], plane_in.at[source],
            a_send.at[to], a_recv.at[source], z * PLANE + to,
        )

    def b_copy(to, source):
        return remote(
            plane_sum.at[pl.ds(to * share, share)], line_in.at[source],
            b_send.at[to], b_recv.at[source], to * PLANE + p,
        )

    def c_copy(to, source):
        there = pl.ds(p * quarter + source * share, share)
        return remote(tri_sum.at[there], tri_sum.at[there], c_send.at[to], c_recv.at[source], to * PLANE + p)

    def d_copy(to, source):
        there = pl.ds(source * quarter, quarter)
        return remote(tri_sum.at[there], tri_sum.at[there], d_send.at[to], d_recv.at[source], z * PLANE + to)

    def gather(first, last):
        @pl.loop(first, last)
        def _(u):
            turn = u // PLANE
            away = line // 2 + ((turn + 1) // 2) * (1 - 2 * lax.rem(turn + 1, 2))
            to = lax.rem(z + away, line) * PLANE + lax.rem(p + u + 1, PLANE)
            rows, counts = block_of(to)
            y_out[to] = rows
            w_out[to] = counts
            y_copy(to, me).start()
            w_copy(to, me).start()

    pl.semaphore_wait(barrier, n - 1)
    in_plane(lambda to: a_copy(to, p).start())
    to_scalars.wait()
    gather(0, n * 3 // 16)

    plane_in[p] = tri[pl.ds(p * quarter, quarter)]
    in_plane(lambda source: a_copy(p, source).wait_recv())
    plane_sum[...] = jnp.sum(plane_in[...], axis=0)
    in_line(lambda to: b_copy(to, z).start(), True)
    gather(n * 3 // 16, n * 6 // 16)

    def reduce():
        line_in[z] = plane_sum[pl.ds(z * share, share)]
        in_line(lambda source: b_copy(z, source).wait_recv())
        tri_sum[pl.ds(p * quarter + z * share, share)] = jnp.sum(line_in[...], axis=0)
        in_line(lambda to: c_copy(to, z).start())

    if_owner(reduce)
    gather(n * 6 // 16, n * 10 // 16)
    in_line(lambda source: c_copy(z, source).wait_recv(), True)
    in_plane(lambda to: d_copy(to, p).start())
    gather(n * 10 // 16, n - 1)
    rows, counts = block_of(me)
    y_in[me] = rows
    w_in[me] = counts

    in_plane(lambda source: d_copy(p, source).wait_recv())
    full = tri_sum[...].reshape(3 * half, half)
    cross = full[half : 2 * half]
    shared = jnp.concatenate(
        [
            jnp.concatenate([full[:half], cross], axis=1),
            jnp.concatenate([cross.T, full[2 * half :]], axis=1),
        ],
        axis=0,
    )
    shared3 = pieces(shared)

    def dense(v, v3):
        wide = add_pieces(nt(v3, shared3))
        return wide[:, :rank] + wide[:, rank : 2 * rank] + wide[:, 2 * rank :] + damping * v

    factors = start[...]
    v3 = pieces(factors)
    residual = -dense(factors, v3)

    def each_other(body):
        @pl.loop(1, n)
        def _(j):
            body(lax.rem(me + j, n))

    def finish_y(source):
        y_copy(me, source).wait_recv()
        w_copy(me, source).wait_recv()

    each_other(finish_y)

    groups = []
    for d in range(0, n, 2):
        groups.append(w_in[d].astype(f32) + pltpu.roll(w_in[d + 1].astype(f32), slots, 1))
    weight = jnp.concatenate(groups, axis=1) * conf_scale
    ys = y_in[...].reshape(n * slots, y_in.shape[2])

    def sparse(v3, target):
        inner = add_pieces(nt(v3, ys))
        coeffs = weight * (1.0 - inner) if target else weight * inner
        return add_pieces(jnp.dot(pieces(coeffs), ys, preferred_element_type=f32))

    residual = sparse(v3, True) + residual
    direction = residual
    norm_now = jnp.sum(residual * residual, axis=1, keepdims=True)
    for sweep in range(ITERS):
        v3 = pieces(direction)
        image = sparse(v3, False) + dense(direction, v3)
        step = norm_now / (jnp.sum(direction * image, axis=1, keepdims=True) + epsilon)
        factors = factors + step * direction
        if sweep + 1 < ITERS:
            residual = residual - step * image
            norm_next = jnp.sum(residual * residual, axis=1, keepdims=True)
            direction = residual + (norm_next / (norm_now + epsilon)) * direction
            norm_now = norm_next
    out[...] = factors

    def sent(to):
        y_copy(to, me).wait_send()
        w_copy(to, me).wait_send()

    each_other(sent)
    in_plane(lambda to: a_copy(to, p).wait_send())
    in_line(lambda to: b_copy(to, z).wait_send(), True)
    if_owner(lambda: in_line(lambda to: c_copy(to, z).wait_send()))
    in_plane(lambda to: d_copy(to, p).wait_send())


def shards(build_factors, nz_build, nz_test, nz_count, start_factors):
    tests, rank = start_factors.shape
    bld_rows = build_factors.shape[0]
    nz_rows = nz_build.shape[0]
    n = lax.axis_size("builds")
    conf_scale = n * bld_rows * tests / (8.0 * nz_rows)
    damping = 0.4 * conf_scale
    slots = tests * MOST
    half = rank // 2
    part = 8
    tiles = 3 * half // part
    line = n // PLANE
    quarter = tiles // PLANE
    owners = max(k for k in range(1, min(line, quarter) + 1) if quarter % k == 0)
    share = quarter // owners
    lump = 16
    chunks = bld_rows // 2048
    lines = n * slots // 128
    dma = pltpu.SemaphoreType.DMA
    return pl.pallas_call(
        functools.partial(kernel, n, owners, conf_scale, damping),
        out_shape=jax.ShapeDtypeStruct((tests, rank), f32),
        in_specs=[pl.BlockSpec(memory_space=pltpu.HBM)] * 5,
        out_specs=pl.BlockSpec(memory_space=pltpu.VMEM),
        scratch_shapes=[
            pltpu.VMEM((1, nz_rows), jnp.int32),
            pltpu.VMEM((1, nz_rows), jnp.int32),
            pltpu.VMEM((1, nz_rows), jnp.int32),
            pltpu.VMEM((tests, rank), f32),
            pltpu.VMEM((bld_rows // lump, lump, rank), bf16),
            pltpu.VMEM((1, nz_rows), jnp.int32),
            pltpu.VMEM((nz_rows, 128), jnp.int32),
            pltpu.VMEM((lines, 128), f32),
            pltpu.VMEM((lines, 128), jnp.int32),
            pltpu.SMEM((lines, 128), jnp.int32),
            pltpu.VMEM((n * slots, lump * lump), bf16),
            pltpu.VMEM((rank, rank), f32),
            pltpu.VMEM((tiles, part, half), f32),
            pltpu.VMEM((PLANE, quarter, part, half), f32),
            pltpu.VMEM((quarter, part, half), f32),
            pltpu.VMEM((line, share, part, half), f32),
            pltpu.VMEM((tiles, part, half), f32),
            pltpu.VMEM((n, slots, rank), bf16),
            pltpu.VMEM((n, slots, rank), bf16),
            pltpu.VMEM((n, tests, 128), bf16),
            pltpu.VMEM((n, tests, 128), bf16),
            dma((chunks,)),
            dma((4,)),
        ]
        + [dma((n,))] * 4
        + [dma((PLANE,))] * 2
        + [dma((line,))] * 4
        + [dma((PLANE,))] * 2,
        compiler_params=pltpu.CompilerParams(
            collective_id=0, has_side_effects=True, vmem_limit_bytes=64 * 1024 * 1024
        ),
    )(
        nz_build[None, :],
        nz_test.reshape(1, nz_rows),
        nz_count[None, :],
        start_factors,
        build_factors.reshape(bld_rows // lump, lump, rank),
    )


def solution(mesh):
    return jax.shard_map(
        shards,
        mesh=mesh,
        in_specs=(
            P("builds", None),
            P(("groups", "builds")),
            P(("groups", "builds"), None),
            P(("groups", "builds")),
            P(("groups", "builds"), None),
        ),
        out_specs=P(("groups", "builds"), None),
        check_vma=False,
    )
```

time: 44.1 us -> 37.7 us (0.85)
  Pallas kernels: 40.4 us -> 36.1 us
  local copies, waits for them, and re-layouts: 3.37 us -> 1.32 us
    pallas_call x1, Pallas kernels: 40.4 us -> 36.1 us  [shards(): pl.pallas_call(functools.partial(kernel, n, owners, conf_scale, damping),...]
    unnamed x9 -> x1, local copies, waits for them, and re-layouts: 3.37 us -> 1.32 us
where the time goes in v3:
time: 37.7 us; the launch traced here: 37.4 us
  Pallas kernels  36.1 us (96%)
  local copies, waits for them, and re-layouts  1.32 us (4%)
    pallas_call x1, Pallas kernels, shards(): pl.pallas_call(functools.partial(kernel, n, owners, conf_scale, damping),...  36.1 us
    unnamed x1, local copies, waits for them, and re-layouts  1.32 us

profile of v3, /device:TPU:0, one launch (start us, length us, event | category | flops | bytes accessed | tf_op | source)
XLA Modules:
  0.0 37.4 jit_solution(2545409498601652260)
XLA Ops:
  0.0 36.1 %shard_map.55 = f32[16,256]{1,0:T(8,128)} custom-call(s32[1,512]{1,0:T(1,128)} %bitcast.5, s32[1,512]{1,0:T(1,128)} %bitcast.6, s32[1,512]{1,0:T(1,128)} %bitcast.7, f32[16,256]{1,0:T(8,128)} %start_hbm.1, bf16[1536,16,256]{2,1,0:T(8,128)(2,1)} %bitcast.4), custom_call_target="tpu_custom_call" | custom-call | tf_op jit(solution)/shard_map/pallas_call | solution.py:331
  36.1 1.3 %copy.7 = f32[16,256]{1,0:T(8,128)} copy(f32[16,256]{1,0:T(8,128)} %shard_map.55) | data formatting | bytes 32768

commit v4 on v3

--- a/solution.py
+++ b/solution.py
@@ -149,17 +149,21 @@
 
     gram[...] = jnp.zeros_like(gram)
 
-    @pl.loop(0, chunks)
+    def add_gram(c):
+        x = x_buf[pl.ds(c * chunk, chunk)].reshape(chunk * lump, rank)
+        gram[...] += tn(x, x)
+
+    early = max(chunks * 5 // 12, chunks - (n - 1))
+    late = chunks - early
+
+    @pl.loop(0, early)
     def _(c):
         load(c).wait()
-        x = x_buf[pl.ds(c * chunk, chunk)].reshape(chunk * lump, rank)
-        gram[...] += tn(x, x)
-
-    per = half // part
-    for i in range(per):
-        tri[i] = gram[i * part : (i + 1) * part, :half]
-        tri[per + i] = gram[i * part : (i + 1) * part, half:]
-        tri[2 * per + i] = gram[half + i * part : half + (i + 1) * part, half:]
+        add_gram(c)
+
+    @pl.loop(early, chunks)
+    def _(c):
+        load(c).wait()
 
     quarter = tiles // PLANE
     share = quarter // owners
@@ -203,7 +207,7 @@
         there = pl.ds(source * quarter, quarter)
         return remote(tri_sum.at[there], tri_sum.at[there], d_send.at[to], d_recv.at[source], z * PLANE + to)
 
-    def gather(first, last):
+    def gather(first, last, with_gram=False):
         @pl.loop(first, last)
         def _(u):
             turn = u // PLANE
@@ -214,17 +218,28 @@
             w_out[to] = counts
             y_copy(to, me).start()
             w_copy(to, me).start()
+            if with_gram:
+                add_gram(early + u)
 
     pl.semaphore_wait(barrier, n - 1)
+    to_scalars.wait()
+    gather(0, late, True)
+
+    per = half // part
+    for i in range(per):
+        tri[i] = gram[i * part : (i + 1) * part, :half]
+        tri[per + i] = gram[i * part : (i + 1) * part, half:]
+        tri[2 * per + i] = gram[half + i * part : half + (i + 1) * part, half:]
+
     in_plane(lambda to: a_copy(to, p).start())
-    to_scalars.wait()
-    gather(0, n * 3 // 16)
+    cuts = [late + (n - 1 - late) * i // 4 for i in range(5)]
+    gather(cuts[0], cuts[1])
 
     plane_in[p] = tri[pl.ds(p * quarter, quarter)]
     in_plane(lambda source: a_copy(p, source).wait_recv())
     plane_sum[...] = jnp.sum(plane_in[...], axis=0)
     in_line(lambda to: b_copy(to, z).start(), True)
-    gather(n * 3 // 16, n * 6 // 16)
+    gather(cuts[1], cuts[2])
 
     def reduce():
         line_in[z] = plane_sum[pl.ds(z * share, share)]
@@ -233,10 +248,10 @@
         in_line(lambda to: c_copy(to, z).start())
 
     if_owner(reduce)
-    gather(n * 6 // 16, n * 10 // 16)
+    gather(cuts[2], cuts[3])
     in_line(lambda source: c_copy(z, source).wait_recv(), True)
     in_plane(lambda to: d_copy(to, p).start())
-    gather(n * 10 // 16, n - 1)
+    gather(cuts[3], cuts[4])
     rows, counts = block_of(me)
     y_in[me] = rows
     w_in[me] = counts

time: 37.7 us -> 36.6 us (0.971)
  Pallas kernels: 36.1 us -> 35 us
    pallas_call x1, Pallas kernels: 36.1 us -> 35 us  [shards(): pl.pallas_call(functools.partial(kernel, n, owners, conf_scale, damping),...]
where the time goes in v4:
time: 36.6 us; the launch traced here: 36.4 us
  Pallas kernels  35 us (96%)
  local copies, waits for them, and re-layouts  1.32 us (4%)
    pallas_call x1, Pallas kernels, shards(): pl.pallas_call(functools.partial(kernel, n, owners, conf_scale, damping),...  35 us
    unnamed x1, local copies, waits for them, and re-layouts  1.32 us

profile of v4, /device:TPU:0, one launch (start us, length us, event | category | flops | bytes accessed | tf_op | source)
XLA Modules:
  0.0 36.4 jit_solution(9181551445858881961)
XLA Ops:
  0.0 35.0 %shard_map.55 = f32[16,256]{1,0:T(8,128)} custom-call(s32[1,512]{1,0:T(1,128)} %bitcast.5, s32[1,512]{1,0:T(1,128)} %bitcast.6, s32[1,512]{1,0:T(1,128)} %bitcast.7, f32[16,256]{1,0:T(8,128)} %start_hbm.1, bf16[1536,16,256]{2,1,0:T(8,128)(2,1)} %bitcast.4), custom_call_target="tpu_custom_call" | custom-call | tf_op jit(solution)/shard_map/pallas_call | solution.py:346
  35.0 1.3 %copy.7 = f32[16,256]{1,0:T(8,128)} copy(f32[16,256]{1,0:T(8,128)} %shard_map.55) | data formatting | bytes 32768

commit v5 on v4

--- a/solution.py
+++ b/solution.py
@@ -9,7 +9,8 @@
 
 ITERS = 3
 MOST = 4
-PLANE = 4
+PLANE = 16
+TURN = 4
 epsilon = 1e-06
 f32 = jnp.float32
 bf16 = jnp.bfloat16
@@ -210,9 +211,9 @@
     def gather(first, last, with_gram=False):
         @pl.loop(first, last)
         def _(u):
-            turn = u // PLANE
-            away = line // 2 + ((turn + 1) // 2) * (1 - 2 * lax.rem(turn + 1, 2))
-            to = lax.rem(z + away, line) * PLANE + lax.rem(p + u + 1, PLANE)
+            turn = u // TURN
+            away = n // TURN // 2 + ((turn + 1) // 2) * (1 - 2 * lax.rem(turn + 1, 2))
+            to = lax.rem(me // TURN + away, n // TURN) * TURN + lax.rem(me + u + 1, TURN)
             rows, counts = block_of(to)
             y_out[to] = rows
             w_out[to] = counts

time: 36.6 us -> 38.3 us (1.046)
  Pallas kernels: 35 us -> 36.7 us
    pallas_call x1, Pallas kernels: 35 us -> 36.7 us  [shards(): pl.pallas_call(functools.partial(kernel, n, owners, conf_scale, damping),...]
where the time goes in v5:
time: 38.3 us; the launch traced here: 38.1 us
  Pallas kernels  36.7 us (96%)
  local copies, waits for them, and re-layouts  1.32 us (3%)
    pallas_call x1, Pallas kernels, shards(): pl.pallas_call(functools.partial(kernel, n, owners, conf_scale, damping),...  36.7 us
    unnamed x1, local copies, waits for them, and re-layouts  1.32 us

profile of v5, /device:TPU:0, one launch (start us, length us, event | category | flops | bytes accessed | tf_op | source)
XLA Modules:
  0.0 38.1 jit_solution(8494852299653066689)
XLA Ops:
  0.0 36.7 %shard_map.55 = f32[16,256]{1,0:T(8,128)} custom-call(s32[1,512]{1,0:T(1,128)} %bitcast.5, s32[1,512]{1,0:T(1,128)} %bitcast.6, s32[1,512]{1,0:T(1,128)} %bitcast.7, f32[16,256]{1,0:T(8,128)} %start_hbm.1, bf16[1536,16,256]{2,1,0:T(8,128)(2,1)} %bitcast.4), custom_call_target="tpu_custom_call" | custom-call | tf_op jit(solution)/shard_map/pallas_call | solution.py:347
  36.7 1.3 %copy.7 = f32[16,256]{1,0:T(8,128)} copy(f32[16,256]{1,0:T(8,128)} %shard_map.55) | data formatting | bytes 32768
